TPU v7x, 256 devices: a whole 4x4x8 slice. The times are simulated.
256 devices in a mesh: slab: 32 (over y, x, core), mem: 8 (over z).
Axes of the slice: x: 4, y: 4, z: 8, core: 2. Of those that a mesh axis runs over, the one named last changes fastest.
Arguments:
- prior_concentrations: float32 [64, 2048, 1024], P('mem', 'slab'), may hold values from -6 to 6
- kappa: float32 [2048, 1024], P('slab'), may hold values from 0.05 to 0.15
- east_face_transport: float32 [2048, 1024], P('slab'), may hold values from -0.08 to 0.08
- v_north: float32 [2048, 1024], P('slab'), may hold values from -0.08 to 0.08
- land: int32 [2048, 1024], P('slab'), may hold values 0 or 1
- obs_owner: int32 [4], replicated, may hold values from 0 to 31, as said below
- obs_offset: int32 [4, 256], replicated, may hold values from 0 to 65535, as said below
- obs_value: float32 [4, 256], replicated, may hold values from -6 to 6
- obs_var: float32 [4, 256], replicated, may hold values from 0.25 to 1
- obs_noise: float32 [4, 256, 64], replicated, may hold values from -6 to 6
Outputs:
- analysis: float32 [64, 2048, 1024], P(None, 'slab', 'mem')
Inputs may be any that keep to these rules, and one draw needn't show every extreme that they name: Batch b observes only rows obs_owner[b] * 64 to obs_owner[b] * 64 + 63. The observed cell lies at row obs_owner * 64 + obs_offset // 1024 and column obs_offset % 1024; cells may repeat.
All inputs are finite; a program needn't handle non-finite values. No bound on the sum of `land` on one device may be relied on, other than what follows from the above.
Results may differ from a plain program's by a relative error of at most 0.00014.
Values sent between devices are 32-bit elements; how exact they have to be, the bound alone decides.
A program may use at most 128 MiB of HBM per device.

v0:
```python
import jax
import jax.numpy as jnp
from jax import lax
from jax.sharding import PartitionSpec as P

STEPS = 2


PRECISE = lax.Precision.HIGHEST


def with_halo(block, sides, width):
    for axis, dim in sides:
        count = lax.axis_size(axis)
        forward = [(i, i + 1) for i in range(count - 1)]
        backward = [(target, source) for source, target in forward]
        low = lax.ppermute(
            lax.slice_in_dim(block, block.shape[dim] - width, None, axis=dim), axis, forward
        )
        high = lax.ppermute(lax.slice_in_dim(block, 0, width, axis=dim), axis, backward)
        block = jnp.concatenate([low, block, high], axis=dim)
    return block


def advance(concentration, static_fields):
    conduct = static_fields[0]
    wetness = static_fields[1]
    eastward = static_fields[2]
    northward = static_fields[3]
    diffuse_east = jnp.sqrt(conduct[:, :-1] * conduct[:, 1:])
    opened_east = wetness[:, :-1] * wetness[:, 1:]
    flow_east = eastward[:, :-1]
    eastward_flux_rows = diffuse_east * (
        concentration[..., :, :-1] - concentration[..., :, 1:]
    ) + opened_east * (
        jnp.maximum(flow_east, 0.0) * concentration[..., :, :-1]
        + jnp.minimum(flow_east, 0.0) * concentration[..., :, 1:]
    )
    diffuse_north = jnp.sqrt(conduct[:-1, :] * conduct[1:, :])
    opened_north = wetness[:-1, :] * wetness[1:, :]
    flow_north = northward[:-1, :]
    flux_north = diffuse_north * (
        concentration[..., :-1, :] - concentration[..., 1:, :]
    ) + opened_north * (
        jnp.maximum(flow_north, 0.0) * concentration[..., :-1, :]
        + jnp.minimum(flow_north, 0.0) * concentration[..., 1:, :]
    )
    change = (
        eastward_flux_rows[..., 1:-1, 1:]
        - eastward_flux_rows[..., 1:-1, :-1]
        + flux_north[..., 1:, 1:-1]
        - flux_north[..., :-1, 1:-1]
    )
    return wetness[1:-1, 1:-1] * (concentration[..., 1:-1, 1:-1] - change)


def solve_batch(priors, observed, variance, perturb):
    members = priors.shape[1]
    deviations = priors - jnp.mean(priors, axis=1, keepdims=True)
    spread = jnp.dot(deviations, deviations.T, precision=PRECISE) / (members - 1) + jnp.diag(
        variance
    )
    misfit = observed[:, None] + jnp.sqrt(variance)[:, None] * perturb - priors
    factor = jnp.linalg.cholesky(spread)
    halfway = lax.linalg.triangular_solve(factor, misfit, left_side=True, lower=True)
    weights = lax.linalg.triangular_solve(
        factor, halfway, left_side=True, lower=True, transpose_a=True
    )
    return (deviations, weights)


def apply_batch(
    states,
    deviations,
    weights,
    row_places,
    column_places,
    site_row,
    site_column,
    wet_flat,
    taper_rate,
):
    members = states.shape[0]
    anomalies = states - jnp.mean(states, axis=0, keepdims=True)
    covariance = jnp.dot(deviations, anomalies, precision=PRECISE) / (members - 1)
    row_gap = (row_places[None, :] - site_row[:, None]).astype(jnp.float32)
    column_gap = (column_places[None, :] - site_column[:, None]).astype(jnp.float32)
    tapering = jnp.exp(-taper_rate * (row_gap * row_gap + column_gap * column_gap))
    return states + jnp.dot(weights.T, tapering * covariance, precision=PRECISE) * wet_flat[None, :]


def regroup(operand):
    return lax.all_to_all(operand, "mem", split_axis=2, concat_axis=0, tiled=True)


def on_device(
    prior_concentrations,
    kappa,
    east_face_transport,
    v_north,
    land,
    obs_owner,
    obs_offset,
    obs_value,
    obs_var,
    obs_noise,
):
    local_lines = prior_concentrations.shape[1]
    padded_width = prior_concentrations.shape[2]
    groups = lax.axis_size("mem")
    narrow = padded_width // groups
    slab_at = lax.axis_index("slab")
    group_at = lax.axis_index("mem")
    wetness = land.astype(jnp.float32)
    static_fields = jnp.stack([wetness * kappa, wetness, east_face_transport, v_north])
    wet_columns = lax.dynamic_slice_in_dim(wetness, group_at * narrow, narrow, 1)
    static_halo = with_halo(static_fields, (("slab", 1),), 1)
    static_halo = jnp.pad(static_halo, ((0, 0), (0, 0), (1, 1)))
    concentration_maps = prior_concentrations
    for step_number in range(STEPS):
        padded = with_halo(concentration_maps, (("slab", 1),), 1)
        concentration_maps = advance(jnp.pad(padded, ((0, 0), (0, 0), (1, 1))), static_halo)
    ensemble = regroup(concentration_maps)
    members = ensemble.shape[0]
    cell_count = local_lines * narrow
    states = ensemble.reshape(members, cell_count)
    wet_flat = wet_columns.reshape(cell_count)
    position = lax.iota(jnp.int32, cell_count)
    row_places = slab_at * local_lines + position // narrow
    column_places = group_at * narrow + position % narrow
    cell_ids = obs_owner[:, None] * (local_lines * padded_width) + obs_offset
    site_rows = cell_ids // padded_width
    site_columns = cell_ids % padded_width
    inside = (site_rows // local_lines == slab_at) & (site_columns // narrow == group_at)
    local_ids = jnp.where(
        inside, (site_rows - slab_at * local_lines) * narrow + site_columns - group_at * narrow, -1
    )
    extent = local_lines * lax.axis_size("slab") // 2
    taper_rate = 0.5 / (extent * extent)
    batches = obs_owner.shape[0]
    for batch_number in range(batches):
        choosing_mask = (local_ids[batch_number][:, None] == position[None, :]).astype(jnp.float32)
        priors = lax.psum(
            lax.dot_general(choosing_mask, states, (((1,), (1,)), ((), ())), precision=PRECISE),
            ("slab", "mem"),
        )
        deviations, weights = solve_batch(
            priors, obs_value[batch_number], obs_var[batch_number], obs_noise[batch_number]
        )
        states = apply_batch(
            states,
            deviations,
            weights,
            row_places,
            column_places,
            site_rows[batch_number],
            site_columns[batch_number],
            wet_flat,
            taper_rate,
        )
    return states.reshape(members, local_lines, narrow)


def solution(mesh):
    placed = (
        P("mem", "slab", None),
        P("slab", None),
        P("slab", None),
        P("slab", None),
        P("slab", None),
        P(),
        P(),
        P(),
        P(),
        P(),
    )
    return jax.shard_map(
        on_device, mesh=mesh, in_specs=placed, out_specs=P(None, "slab", "mem"), check_vma=False
    )
```

profile of v0, /device:TPU:6, one launch (start us, length us, event | category | flops | bytes accessed | tf_op | source)
XLA Modules:
  0.0 1420.6 jit_solution(12570317617643870160)
XLA Ops:
  66.2 51.9 %all-to-all-done = f32[8,1,65536]{2,1,0:T(1,128)S(1)} async-done(((f32[8,1,65536]{2,1,0:T(1,128)}), f32[8,1,65536]{2,1,0:T(1,128)S(1)}, u32[]{:S(2)}, u32[]{:S(2)}) %all-to-all-start) | async-done | bytes 2097184 | tf_op jit(solution)/shard_map/all_to_all | solution.py:93
  148.6 223.3 %all-reduce.9.cloned.1.call-done = f32[256,64]{0,1:T(8,128)} async-done(((f32[256,64]{0,1:T(8,128)}), f32[256,64]{0,1:T(8,128)}) %all-reduce.9.cloned.1.call-update) | async-done | bytes 65552 | tf_op jit(solution)/shard_map/psum | solution.py:143
  374.3 11.7 cholesky.214
  386.1 9.8 custom-call.23
  396.4 11.7 cholesky.231
  414.7 20.1 %custom-call.25 = f32[2,128,128]{1,2,0:T(8,128)S(1)} custom-call(f32[2,128,128]{2,1,0:T(8,128)S(1)} %get-tuple-element.61), custom_call_target="InvertDiagBlocksLowerTriangular" | custom-call | tf_op jit(solution)/shard_map/triangular_solve/custom-call.4 | solution.py:66
  436.1 9.8 fusion.3
  457.9 234.1 %all-reduce.11.cloned.1.call-done = f32[256,64]{0,1:T(8,128)} async-done(((f32[256,64]{0,1:T(8,128)}), f32[256,64]{0,1:T(8,128)}) %all-reduce.11.cloned.1.call-update) | async-done | bytes 65552 | tf_op jit(solution)/shard_map/psum | solution.py:143
  694.4 11.7 cholesky.248
  706.2 9.8 custom-call.26
  716.5 11.7 cholesky.265
  734.8 20.1 %custom-call.28 = f32[2,128,128]{1,2,0:T(8,128)S(1)} custom-call(f32[2,128,128]{2,1,0:T(8,128)S(1)} %get-tuple-element.63), custom_call_target="InvertDiagBlocksLowerTriangular" | custom-call | tf_op jit(solution)/shard_map/triangular_solve/custom-call.4 | solution.py:66
  756.2 9.8 fusion.2
  777.9 234.2 %all-reduce.13.cloned.1.call-done = f32[256,64]{0,1:T(8,128)} async-done(((f32[256,64]{0,1:T(8,128)}), f32[256,64]{0,1:T(8,128)}) %all-reduce.13.cloned.1.call-update) | async-done | bytes 65552 | tf_op jit(solution)/shard_map/psum | solution.py:143
  1014.5 11.7 cholesky.282
  1026.3 9.8 custom-call.29
  1036.6 11.7 cholesky.299
  1054.9 20.1 %custom-call.31 = f32[2,128,128]{1,2,0:T(8,128)S(1)} custom-call(f32[2,128,128]{2,1,0:T(8,128)S(1)} %get-tuple-element.65), custom_call_target="InvertDiagBlocksLowerTriangular" | custom-call | tf_op jit(solution)/shard_map/triangular_solve/custom-call.4 | solution.py:66
  1076.3 9.8 fusion.1
  1098.0 234.4 %all-reduce.15.cloned.1.call-done = f32[256,64]{0,1:T(8,128)} async-done(((f32[256,64]{0,1:T(8,128)}), f32[256,64]{0,1:T(8,128)}) %all-reduce.15.cloned.1.call-update) | async-done | bytes 65552 | tf_op jit(solution)/shard_map/psum | solution.py:143
  1334.8 11.7 cholesky.316
  1346.6 10.0 custom-call.32
  1357.1 11.7 cholesky.333
  1375.4 19.9 %custom-call.34 = f32[2,128,128]{1,2,0:T(8,128)S(1)} custom-call(f32[2,128,128]{2,1,0:T(8,128)S(1)} %get-tuple-element.67), custom_call_target="InvertDiagBlocksLowerTriangular" | custom-call | tf_op jit(solution)/shard_map/triangular_solve/custom-call.4 | solution.py:66
  (226 shorter events, 195.9 us)
Async XLA Ops:
  9.6 12.6 copy-start.8
  9.6 12.6 copy-start.9
  9.6 12.5 collective-permute-start
  11.7 10.5 collective-permute-start.1
  16.6 6.8 collective-permute-start.2
  18.5 6.3 collective-permute-start.3
  29.5 8.8 collective-permute-start.4
  36.1 3.5 collective-permute-start.5
  56.9 9.1 copy-start.18
  56.9 9.1 copy-start.17
  56.9 9.2 copy-start.15
  56.9 61.2 %all-to-all-start = ((f32[8,1,65536]{2,1,0:T(1,128)}), f32[8,1,65536]{2,1,0:T(1,128)S(1)}, u32[]{:S(2)}, u32[]{:S(2)}) async-start(f32[8,1,65536]{2,1,0:T(1,128)} %reshape.235), calls=%async_computation | async-start | bytes 4194304 | tf_op jit(solution)/shard_map/all_to_all | solution.py:93
  65.5 306.4 %all-reduce.9.cloned.1.call-start = ((), (), s32[]{:S(2)}) async-start(), calls=%async_computation.1 | async-start | bytes 131072 | tf_op jit(solution)/shard_map/psum | solution.py:143
  133.7 238.1 %copy-start.10 = (f32[4,256,64]{1,2,0:T(8,128)S(1)}, f32[4,256,64]{1,2,0:T(8,128)}, u32[]{:S(2)}) copy-start(f32[4,256,64]{1,2,0:T(8,128)} %param.24) | copy-start | bytes 786436
  139.1 552.9 %all-reduce.11.cloned.1.call-start = ((), (), s32[]{:S(2)}) async-start(), calls=%async_computation.2 | async-start | bytes 131072 | tf_op jit(solution)/shard_map/psum | solution.py:143
  374.1 62.1 %copy-start.12 = (f32[256,64]{0,1:T(8,128)S(1)}, f32[256,64]{0,1:T(8,128)}, u32[]{:S(2)}) copy-start(f32[256,64]{0,1:T(8,128)} %all-reduce.9.cloned.1.call-done) | copy-start | bytes 196612
  457.8 554.3 %all-reduce.13.cloned.1.call-start = ((), (), s32[]{:S(2)}) async-start(), calls=%async_computation.3 | async-start | bytes 131072 | tf_op jit(solution)/shard_map/psum | solution.py:143
  694.2 62.0 %copy-start.1 = (f32[64,8192]{1,0:T(8,128)S(1)}, f32[64,8192]{1,0:T(8,128)}, u32[]{:S(2)}) copy-start(f32[64,8192]{1,0:T(8,128)} %copy-done) | copy-start | bytes 6291460
  694.2 62.0 %copy-start.13 = (f32[256,64]{0,1:T(8,128)S(1)}, f32[256,64]{0,1:T(8,128)}, u32[]{:S(2)}) copy-start(f32[256,64]{0,1:T(8,128)} %all-reduce.11.cloned.1.call-done) | copy-start | bytes 196612
  777.9 554.5 %all-reduce.15.cloned.1.call-start = ((), (), s32[]{:S(2)}) async-start(), calls=%async_computation.4 | async-start | bytes 131072 | tf_op jit(solution)/shard_map/psum | solution.py:143
  1014.3 62.0 %copy-start.3 = (f32[64,8192]{1,0:T(8,128)S(1)}, f32[64,8192]{1,0:T(8,128)}, u32[]{:S(2)}) copy-start(f32[64,8192]{1,0:T(8,128)} %copy-done.2) | copy-start | bytes 6291460
  1014.3 62.0 %copy-start.14 = (f32[256,64]{0,1:T(8,128)S(1)}, f32[256,64]{0,1:T(8,128)}, u32[]{:S(2)}) copy-start(f32[256,64]{0,1:T(8,128)} %all-reduce.13.cloned.1.call-done) | copy-start | bytes 196612
  1334.6 62.0 %copy-start.6 = (f32[64,8192]{1,0:T(8,128)S(1)}, f32[64,8192]{1,0:T(8,128)}, u32[]{:S(2)}) copy-start(f32[64,8192]{1,0:T(8,128)} %copy-done.5) | copy-start | bytes 6291460
  1334.6 62.0 %copy-start.11 = (f32[256,64]{0,1:T(8,128)S(1)}, f32[256,64]{0,1:T(8,128)}, u32[]{:S(2)}) copy-start(f32[256,64]{0,1:T(8,128)} %all-reduce.15.cloned.1.call-done) | copy-start | bytes 196612
  (6 other events, 23.1 us)
Sparse Core Ops, SparseCore 0:
  139.2 232.5 all-reduce.8
  457.9 234.0 all-reduce.10
  778.0 234.0 all-reduce.12
  1098.1 234.2 all-reduce.14
where the time goes:
time: 1430 us; the launch traced here: 1420 us
  waiting for transfers between devices  981 us (69%)
  other arithmetic  244 us (17%)
  matrix products  93.6 us (7%)
  local copies, waits for them, and re-layouts  43.3 us (3%)
  starting transfers between devices  38.5 us (3%)
  between operations  19.8 us (1%)
    psum x4, waiting for transfers between devices, on_device(): lax.psum(lax.dot_general(choosing_mask, states, (((1,), (1,)), ((), ())),...  926 us
    another operation x28, other arithmetic, solve_batch(): factor = jnp.linalg.cholesky(spread)  139 us
    another operation x9, other arithmetic, solve_batch(): lax.linalg.triangular_solve(factor, halfway, left_side=True, lower=True,...  80.3 us
    all_to_all x1, waiting for transfers between devices, regroup(): lax.all_to_all(operand, 'mem', split_axis=2, concat_axis=0, tiled=True)  51.9 us
    dot_general x4, matrix products, apply_batch(): jnp.dot(deviations, anomalies, precision=PRECISE) / (members - 1)  39 us
  transfers between devices with their start and end apart: 11, of which 7 were waited for; matrix products, arithmetic and copies ran while one was open for 0% of the time, Pallas kernels for 0%

commit v1 on v0

v1 whole, which is shorter than its diff:
```python
import functools

import jax
import jax.numpy as jnp
from jax import lax
from jax.experimental import pallas as pl
from jax.experimental.pallas import tpu as pltpu
from jax.sharding import PartitionSpec as P

F32 = jnp.float32
BF16 = jnp.bfloat16
PRECISE = lax.Precision.HIGHEST
MESH = pl.DeviceIdType.MESH
LANES = 128
OWN = 8
BASE = 8


def contract(a, b, dims):
    return lax.dot_general(
        a, b, ((dims[:1], dims[1:]), ((), ())), precision=PRECISE, preferred_element_type=F32
    )


def quick(a, b):
    return jnp.dot(a, b, preferred_element_type=F32)


def split(x):
    high = x.astype(BF16)
    return high, (x - high.astype(F32)).astype(BF16)


def solve_spd(system):
    rows, lanes = system.shape
    at = lax.broadcasted_iota(jnp.int32, (8, lanes), 0)

    def block(_, parts):
        parts = list(parts)
        for k in range(8):
            head = parts[0]
            factors = [jnp.broadcast_to(p[:, k : k + 1], p.shape) for p in parts]
            pivot = head[k : k + 1, :] / factors[0][k : k + 1, :]
            parts = [p - f * pivot for p, f in zip(parts, factors)]
            parts[0] = jnp.where(at == k, pivot, parts[0])
        parts = [pltpu.roll(p, lanes - 8, 1) for p in parts]
        return tuple(parts[1:] + parts[:1])

    parts = tuple(system[8 * i : 8 * i + 8] for i in range(rows // 8))
    parts = lax.fori_loop(0, rows // 8, block, parts)
    return jnp.concatenate(parts, 0)[:, :rows]


def kernel(
    geometry,
    prior_ref,
    kappa_ref,
    east_ref,
    north_ref,
    land_ref,
    owner_ref,
    offset_ref,
    value_ref,
    var_ref,
    noise_ref,
    out_ref,
    padded,
    middle,
    forecast,
    states,
    stat_send,
    stat_recv,
    ext,
    coef,
    parts,
    column_of,
    line_of,
    sea,
    picked,
    reduce_buf,
    piece,
    gathered,
    sites,
    tapers,
    base_misfit,
    dcat,
    wcat,
    column_taper,
    row_site,
    wet_cols,
    site_cols,
    halo_send,
    halo_recv,
    reduce_send,
    reduce_recv,
    ring_send,
    ring_recv,
    share_send,
    share_recv,
    swap_send,
    swap_recv,
):
    n_slab, n_mem, n_piece, rb = geometry
    rows = kappa_ref.shape[0]
    width = kappa_ref.shape[1]
    members = OWN * n_mem
    batches, nobs = var_ref.shape
    total_obs = batches * nobs
    chunks = rows // rb
    extent = rows * n_slab // 2
    rate = 0.5 / (extent * extent)

    s = lax.axis_index("slab")
    z = lax.axis_index("mem")
    mine = lax.rem(s, n_piece)

    def slab_of(d):
        return lax.rem(s + d, n_slab)

    def mem_of(d):
        return lax.rem(z + d, n_mem)

    def piece_of(d):
        return s - mine + lax.rem(mine + d, n_piece)

    barrier = pltpu.get_barrier_semaphore()
    for d in range(1, n_slab):
        pl.semaphore_signal(barrier, inc=1, device_id=(slab_of(d), z), device_id_type=MESH)
    for d in range(1, n_mem):
        pl.semaphore_signal(barrier, inc=1, device_id=(s, mem_of(d)), device_id_type=MESH)

    def fill(r):
        tile = prior_ref[:, pl.ds(r, 8), :]
        padded[pl.ds(r + 2, 8)] = jnp.swapaxes(tile, 0, 1)

    wet = land_ref[...].astype(F32)
    ext[0, BASE : BASE + rows] = wet * kappa_ref[...]
    ext[1, BASE : BASE + rows] = wet
    ext[2, BASE : BASE + rows] = east_ref[...]
    ext[3, BASE : BASE + rows] = north_ref[...]
    for side, first in ((0, BASE), (1, BASE + rows - 2)):
        for field in range(4):
            stat_send[side, 2 * field : 2 * field + 2] = ext[field, first : first + 2]
    fill(0)
    fill(rows - 8)

    pl.semaphore_wait(barrier, n_slab - 1 + n_mem - 1)

    halo = []
    for side, (d, src, dst) in enumerate(
        ((n_slab - 1, 2, rows + 2), (1, rows, 0))
    ):
        target = (slab_of(d), z)
        halo.append(
            pltpu.make_async_remote_copy(
                src_ref=stat_send.at[side],
                dst_ref=stat_recv.at[side],
                send_sem=halo_send.at[2 * side],
                recv_sem=halo_recv.at[2 * side],
                device_id=target,
                device_id_type=MESH,
            )
        )
        halo.append(
            pltpu.make_async_remote_copy(
                src_ref=padded.at[pl.ds(src, 2)],
                dst_ref=padded.at[pl.ds(dst, 2)],
                send_sem=halo_send.at[2 * side + 1],
                recv_sem=halo_recv.at[2 * side + 1],
                device_id=target,
                device_id_type=MESH,
            )
        )
    for copy in halo:
        copy.start()

    def fill_rest(i, carry):
        fill(pl.multiple_of(8 * i, 8))
        return carry

    lax.fori_loop(1, rows // 8 - 1, fill_rest, 0)

    offsets = offset_ref[...]
    batch_at = lax.broadcasted_iota(jnp.int32, offsets.shape, 0)
    owner_rows = jnp.zeros(offsets.shape, jnp.int32)
    for b in range(batches):
        owner_rows = jnp.where(batch_at == b, owner_ref[b] * rows, owner_rows)
    site_row = (owner_rows + offsets // width).astype(F32)
    site_col = (offsets % width).astype(F32)
    sites[0:batches] = site_row
    sites[batches : 2 * batches] = site_col
    flipped = sites[...].T
    row0 = (s * rows).astype(F32)
    col0 = (z * LANES).astype(F32)
    columns = lax.broadcasted_iota(jnp.int32, (1, LANES), 1).astype(F32) + col0
    for b in range(batches):
        row_j = flipped[:, b : b + 1]
        col_j = flipped[:, batches + b : batches + b + 1]
        gap = col_j - columns
        column_taper[b] = jnp.exp(-rate * (gap * gap))
        row_site[b] = jnp.broadcast_to(row_j, (nobs, LANES)) - row0
        for later in range(b + 1, batches):
            g_row = row_j - sites[later : later + 1]
            g_col = col_j - sites[batches + later : batches + later + 1]
            tapers[b, :, nobs * later : nobs * (later + 1)] = jnp.exp(
                -rate * (g_row * g_row + g_col * g_col)
            )
        base_misfit[b] = (
            value_ref[b : b + 1] + jnp.sqrt(var_ref[b : b + 1]) * noise_ref[b].T
        )
    line_of[...] = jnp.where(owner_rows == s * rows, offsets // width, -1)
    for b in range(batches):
        column = (offsets % width)[b : b + 1]
        for first in range(0, width, nobs):
            at = lax.broadcasted_iota(jnp.int32, (nobs, nobs), 0) + first
            column_of[b, first : first + nobs] = (at == column).astype(F32).astype(BF16)
    sea[...] = wet.astype(BF16)
    wet_cols[...] = land_ref[:, pl.ds(pl.multiple_of(z * LANES, LANES), LANES)].astype(F32)

    for copy in halo:
        copy.wait()

    low_ok = (s > 0).astype(F32)
    high_ok = (s < n_slab - 1).astype(F32)
    for field in range(4):
        ext[field, BASE - 2 : BASE] = stat_recv[1, 2 * field : 2 * field + 2] * low_ok
        ext[field, BASE + rows : BASE + rows + 2] = (
            stat_recv[0, 2 * field : 2 * field + 2] * high_ok
        )

    tall = ext.shape[1]
    lane = lax.broadcasted_iota(jnp.int32, (1, width), 1)
    not_last = (lane < width - 1).astype(F32)
    not_first = (lane > 0).astype(F32)

    def coefficients(first, count):
        conduct, open_, east, north = (ext[f, first : first + count + 2] for f in range(4))

        def leave_enter(near, near_open, far, far_open, flow):
            diffuse = jnp.sqrt(near * far)
            opened = near_open * far_open
            return (
                diffuse + opened * jnp.maximum(flow, 0.0),
                diffuse - opened * jnp.minimum(flow, 0.0),
            )

        mid = slice(1, count + 1)
        c, o = conduct[mid], open_[mid]
        c_next = pltpu.roll(c, width - 1, 1) * not_last
        o_next = pltpu.roll(o, width - 1, 1) * not_last
        out_e, in_e = leave_enter(c, o, c_next, o_next, east[mid])
        out_w = pltpu.roll(out_e, 1, 1) * not_first
        in_w = pltpu.roll(in_e, 1, 1) * not_first
        out_n, in_n = leave_enter(
            conduct[: count + 1], open_[: count + 1], conduct[1:], open_[1:], north[: count + 1]
        )
        where = slice(first + 1, first + 1 + count)
        coef[0, where] = o * (1.0 - out_e - in_w - out_n[1:] - in_n[:-1])
        coef[1, where] = o * in_e
        coef[2, where] = o * out_w
        coef[3, where] = o * in_n[1:]
        coef[4, where] = o * out_n[:-1]

    for first in range(0, rows, 8):
        coefficients(BASE - 1 + first, 8)
    coefficients(BASE - 2, 1)
    coefficients(BASE + rows - 1, 1)

    def stencil(source, at, row):
        def c(i):
            return jnp.broadcast_to(coef[i, pl.ds(row + BASE, 1), :], (OWN, width))

        here = source[at]
        return (
            c(0) * here
            + c(1) * pltpu.roll(here, width - 1, 1)
            + c(2) * pltpu.roll(here, 1, 1)
            + c(3) * source[at + 1]
            + c(4) * source[at - 1]
        )

    def first_step(i, carry):
        middle[i] = stencil(padded, i + 1, i - 1)
        return carry

    def second_step(i, carry):
        r = 2 * i
        pair = [stencil(middle, r + 1 + q, r + q) for q in range(2)]
        for q in range(2):
            forecast[r + q] = pair[q]
        value = jnp.concatenate(pair, 0)
        high = value.astype(BF16)
        rest = value - high.astype(F32)
        middle_part, low = split(rest)
        spot = pl.ds(pl.multiple_of(i * 2 * OWN, 2 * OWN), 2 * OWN)
        parts[0, spot] = high
        parts[1, spot] = middle_part
        parts[2, spot] = low
        return carry

    lax.fori_loop(0, rows + 2, first_step, 0, unroll=2)
    lax.fori_loop(0, rows // 2, second_step, 0)

    swaps = []
    for chunk in range(chunks):
        for d in range(1, n_mem):
            t = mem_of(d)
            swaps.append(
                pltpu.make_async_remote_copy(
                    src_ref=forecast.at[
                        pl.ds(chunk * rb, rb), :, pl.ds(pl.multiple_of(t * LANES, LANES), LANES)
                    ],
                    dst_ref=states.at[
                        pl.ds(chunk * rb, rb), pl.ds(pl.multiple_of(z * OWN, OWN), OWN), :
                    ],
                    send_sem=swap_send.at[chunk * n_mem + d],
                    recv_sem=swap_recv.at[chunk * n_mem + d],
                    device_id=(s, t),
                    device_id_type=MESH,
                )
            )
    for copy in swaps:
        copy.start()
    states[:, pl.ds(pl.multiple_of(z * OWN, OWN), OWN), :] = forecast[
        :, :, pl.ds(pl.multiple_of(z * LANES, LANES), LANES)
    ]

    per_batch = nobs // LANES

    def pick_batch(b, carry):
        line = line_of[pl.ds(b, 1), :]
        chosen_column = column_of[b]
        tracer = jnp.zeros((OWN, nobs), F32)
        for part in range(3):
            tracer_part = quick(parts[part], chosen_column).reshape(rows, OWN, nobs)
            for r in range(rows):
                tracer = tracer + jnp.where(line == r, tracer_part[r], 0.0)
        sea_part = quick(sea[...], chosen_column)
        at_row = lax.broadcasted_iota(jnp.int32, (rows, nobs), 0)
        found = jnp.sum(jnp.where(line == at_row, sea_part, 0.0), axis=0, keepdims=True)
        for q in range(per_batch):
            lanes = slice(LANES * q, LANES * (q + 1))
            picked[b * per_batch + q, 0:OWN] = tracer[:, lanes]
            picked[b * per_batch + q, OWN : 2 * OWN] = jnp.broadcast_to(
                found[:, lanes], (OWN, LANES)
            )
        return carry

    lax.fori_loop(0, batches, pick_batch, 0)

    reduces = []
    for d in range(1, n_slab):
        t = slab_of(d)
        reduces.append(
            pltpu.make_async_remote_copy(
                src_ref=picked.at[lax.rem(t, n_piece)],
                dst_ref=reduce_buf.at[d],
                send_sem=reduce_send.at[d],
                recv_sem=reduce_recv.at[d],
                device_id=(t, z),
                device_id_type=MESH,
            )
        )
    for copy in reduces:
        copy.start()
    total = picked[mine]
    for d, copy in enumerate(reduces, 1):
        copy.wait_recv()
        total = total + reduce_buf[d]
    piece[...] = total

    own_rows = pl.ds(pl.multiple_of(z * OWN, OWN), OWN)
    rings = []
    for d in range(1, n_mem):
        rings.append(
            pltpu.make_async_remote_copy(
                src_ref=piece.at[pl.ds(0, OWN)],
                dst_ref=gathered.at[own_rows],
                send_sem=ring_send.at[d],
                recv_sem=ring_recv.at[d],
                device_id=(s, mem_of(d)),
                device_id_type=MESH,
            )
        )
    for copy in rings:
        copy.start()
    gathered[own_rows] = total[0:OWN]
    gathered[members : members + OWN] = total[OWN : 2 * OWN]
    for copy in rings:
        copy.wait_recv()

    own_lanes = pl.ds(pl.multiple_of(mine * LANES, LANES), LANES)
    shares = []
    for d in range(1, n_piece):
        shares.append(
            pltpu.make_async_remote_copy(
                src_ref=gathered,
                dst_ref=site_cols.at[:, own_lanes],
                send_sem=share_send.at[d],
                recv_sem=share_recv.at[d],
                device_id=(piece_of(d), z),
                device_id_type=MESH,
            )
        )
    for copy in shares:
        copy.start()
    site_cols[:, own_lanes] = gathered[...]
    for copy in shares:
        copy.wait_recv()

    eye = (
        lax.broadcasted_iota(jnp.int32, (members, 2 * members), 0)
        == lax.broadcasted_iota(jnp.int32, (members, 2 * members), 1)
    ).astype(F32)
    for b in range(batches):
        now = slice(nobs * b, nobs * (b + 1))
        priors = site_cols[0:members, now]
        deviations = priors - jnp.mean(priors, axis=0, keepdims=True)
        inverse_var = 1.0 / var_ref[b : b + 1]
        misfit = base_misfit[b] - priors
        system = contract(
            deviations * inverse_var, jnp.concatenate([deviations, misfit], 0), (1, 1)
        ) + eye * (members - 1.0)
        solved = solve_spd(system)
        weights = (misfit - contract(solved, deviations, (0, 0))) * (
            inverse_var * (1.0 / (members - 1))
        )
        high, low = split(deviations.T)
        dcat[b] = jnp.concatenate([high, high, low], 1)
        high, low = split(weights)
        wcat[b] = jnp.concatenate([high, low], 0)
        if b < batches - 1:
            rest = slice(nobs * (b + 1), total_obs)
            values = site_cols[0:members, rest]
            anomalies = values - jnp.mean(values, axis=0, keepdims=True)
            covariance = contract(deviations, anomalies, (0, 0))
            site_cols[0:members, rest] = (
                values
                + contract(weights, tapers[b, :, rest] * covariance, (1, 0))
                * site_cols[members : members + 1, rest]
            )

    for chunk in range(chunks):
        for copy in swaps[chunk * (n_mem - 1) : (chunk + 1) * (n_mem - 1)]:
            copy.wait_recv()
        first = chunk * rb
        wet_here = jnp.concatenate([wet_cols[first + q : first + q + 1] for q in range(rb)], 1)
        here = jnp.concatenate([states[first + q] for q in range(rb)], 1)

        def assimilate(b, here):
            anomalies = here - jnp.mean(here, axis=0, keepdims=True)
            high, low = split(anomalies)
            covariance = quick(dcat[b], jnp.concatenate([high, low, high], 0))
            taper = []
            for q in range(rb):
                gap = row_site[b] - float(first + q)
                taper.append(jnp.exp(-rate * (gap * gap)) * column_taper[b])
            high, low = split(covariance * jnp.concatenate(taper, 1))
            both = quick(wcat[b], high)
            change = both[:members] + both[members:] + quick(wcat[b, 0:members], low)
            return here + change * wet_here

        here = lax.fori_loop(0, batches, assimilate, here)
        for q in range(rb):
            out_ref[pl.ds(first + q, members, stride=rows), :] = here[
                :, LANES * q : LANES * (q + 1)
            ]

    for copy in swaps + reduces + rings + shares:
        copy.wait_send()


def geometry_of(mesh_shape, rows, batches, nobs):
    n_piece = batches * nobs // LANES
    return mesh_shape["slab"], mesh_shape["mem"], n_piece, min(16, rows // 2)


def on_device(
    geometry,
    prior_concentrations,
    kappa,
    east_face_transport,
    v_north,
    land,
    obs_owner,
    obs_offset,
    obs_value,
    obs_var,
    obs_noise,
):
    n_slab, n_mem, n_piece, rb = geometry
    own, rows, width = prior_concentrations.shape
    batches, nobs = obs_value.shape
    members = own * n_mem
    chunks = rows // rb
    tall = rows + 2 * BASE
    vmem = pl.BlockSpec(memory_space=pltpu.VMEM)
    smem = pl.BlockSpec(memory_space=pltpu.SMEM)
    dma = pltpu.SemaphoreType.DMA
    out = pl.pallas_call(
        functools.partial(kernel, geometry),
        out_shape=jax.ShapeDtypeStruct((members * rows, LANES), F32),
        in_specs=[vmem] * 5 + [smem] + [vmem] * 4,
        out_specs=vmem,
        scratch_shapes=[
            pltpu.VMEM((rows + 4, own, width), F32),
            pltpu.VMEM((rows + 2, own, width), F32),
            pltpu.VMEM((rows, own, width), F32),
            pltpu.VMEM((rows, members, LANES), F32),
            pltpu.VMEM((2, 8, width), F32),
            pltpu.VMEM((2, 8, width), F32),
            pltpu.VMEM((4, tall, width), F32),
            pltpu.VMEM((5, tall, width), F32),
            pltpu.VMEM((3, rows * own, width), BF16),
            pltpu.VMEM((batches, width, nobs), BF16),
            pltpu.VMEM((batches, nobs), jnp.int32),
            pltpu.VMEM((rows, width), BF16),
            pltpu.VMEM((n_piece, 2 * own, LANES), F32),
            pltpu.VMEM((n_slab, 2 * own, LANES), F32),
            pltpu.VMEM((2 * own, LANES), F32),
            pltpu.VMEM((members + own, LANES), F32),
            pltpu.VMEM((2 * batches, nobs), F32),
            pltpu.VMEM((batches - 1, nobs, batches * nobs), F32),
            pltpu.VMEM((batches, members, nobs), F32),
            pltpu.VMEM((batches, nobs, 3 * members), BF16),
            pltpu.VMEM((batches, 2 * members, nobs), BF16),
            pltpu.VMEM((batches, nobs, LANES), F32),
            pltpu.VMEM((batches, nobs, LANES), F32),
            pltpu.VMEM((rows, LANES), F32),
            pltpu.VMEM((members + own, batches * nobs), F32),
            dma((4,)),
            dma((4,)),
            dma((n_slab,)),
            dma((n_slab,)),
            dma((n_mem,)),
            dma((n_mem,)),
            dma((n_piece,)),
            dma((n_piece,)),
            dma((chunks * n_mem,)),
            dma((chunks * n_mem,)),
        ],
        compiler_params=pltpu.CompilerParams(
            collective_id=0, has_side_effects=True, vmem_limit_bytes=48 << 20
        ),
    )(
        prior_concentrations,
        kappa,
        east_face_transport,
        v_north,
        land,
        obs_owner,
        obs_offset,
        obs_value,
        obs_var,
        obs_noise,
    )
    return out.reshape(members, rows, LANES)


def solution(mesh):
    placed = (
        P("mem", "slab", None),
        P("slab", None),
        P("slab", None),
        P("slab", None),
        P("slab", None),
        P(),
        P(),
        P(),
        P(),
        P(),
    )

    def whole(*arguments):
        prior, value = arguments[0], arguments[7]
        rows = prior.shape[1] // mesh.shape["slab"]
        geometry = geometry_of(mesh.shape, rows, *value.shape)
        return jax.shard_map(
            functools.partial(on_device, geometry),
            mesh=mesh,
            in_specs=placed,
            out_specs=P(None, "slab", "mem"),
            check_vma=False,
        )(*arguments)

    return whole
```

time: 1430 us -> 141 us (0.10)
  the two profiles are of different devices: /device:TPU:6 before, /device:TPU:1 now
where the time goes in v1:
time: 141 us; the launch traced here: 140 us
  Pallas kernels  130 us (92%)
  local copies, waits for them, and re-layouts  10.6 us (8%)
    pallas_call x1, Pallas kernels, on_device(): pl.pallas_call(functools.partial(kernel, geometry), out_shape=jax.ShapeDt...  130 us
    unnamed x20, local copies, waits for them, and re-layouts  10.6 us

profile of v1, /device:TPU:1, one launch (start us, length us, event | category | flops | bytes accessed | tf_op | source)
XLA Modules:
  0.0 140.4 jit_solution(9623811883148774846)
XLA Ops:
  0.0 1.1 copy.11.noise_ref
  1.2 0.0 copy-start
  1.2 1.6 %copy-done = f32[8,64,1024]{2,1,0:T(8,128)S(1)} copy-done((f32[8,64,1024]{2,1,0:T(8,128)S(1)}, f32[8,64,1024]{2,1,0:T(8,128)}, u32[]{:S(2)}) %copy-start) | copy-done | bytes 2097176
  2.7 0.0 copy-start.1
  2.8 0.9 copy-done.1
  3.7 0.0 copy-start.2
  3.7 0.9 copy-done.2
  4.6 0.0 copy-start.3
  4.7 0.9 copy-done.3
  5.6 0.0 copy-start.4
  5.6 0.9 copy-done.4
  6.5 0.0 copy-start.5
  6.6 0.7 copy-done.5
  7.2 0.0 copy-start.6
  7.2 0.7 copy-done.6
  7.9 0.0 copy-start.7
  7.9 0.7 copy-done.7
  8.6 0.0 copy-start.8
  8.6 0.7 copy-done.8
  9.3 129.8 %shard_map.100 = f32[4096,128]{1,0:T(8,128)S(1)} custom-call(f32[8,64,1024]{2,1,0:T(8,128)S(1)} %copy-done, f32[64,1024]{1,0:T(8,128)S(1)} %copy-done.1, f32[64,1024]{1,0:T(8,128)S(1)} %copy-done.2, f32[64,1024]{1,0:T(8,128)S(1)} %copy-done.3, s32[64,1024]{1,0:T(8,128)S(1)} %copy-done.4, s32[4]{0:T(128)S(1)} %copy-done.8, s32[4,256]{1,0:T(4,128)S(1)} %copy-done.5, ...), custom_call_target="tpu_custom_call" | custom-call | tf_op jit(solution)/shard_map/pallas_call | solution.py:500
  139.1 1.3 copy.13
Async XLA Ops:
  1.2 1.6 %copy-start = (f32[8,64,1024]{2,1,0:T(8,128)S(1)}, f32[8,64,1024]{2,1,0:T(8,128)}, u32[]{:S(2)}) copy-start(f32[8,64,1024]{2,1,0:T(8,128)} %prior_ref.1) | copy-start | bytes 6291460
  2.7 0.9 copy-start.1
  3.7 0.9 copy-start.2
  4.6 0.9 copy-start.3
  5.6 0.9 copy-start.4
  6.5 0.7 copy-start.5
  7.2 0.7 copy-start.6
  7.9 0.7 copy-start.7
  8.6 0.7 copy-start.8

commit v2 on v1

--- a/solution.py
+++ b/solution.py
@@ -1,4 +1,5 @@
 import functools
+import math
 
 import jax
 import jax.numpy as jnp
@@ -13,6 +14,7 @@
 MESH = pl.DeviceIdType.MESH
 LANES = 128
 OWN = 8
+EARLY = 1
 BASE = 8
 
 
@@ -35,16 +37,28 @@
     rows, lanes = system.shape
     at = lax.broadcasted_iota(jnp.int32, (8, lanes), 0)
 
+    def wide(x):
+        return jnp.broadcast_to(x, (8, lanes))
+
     def block(_, parts):
-        parts = list(parts)
+        head, others = parts[0], parts[1:]
+        columns = [wide(head[:, k : k + 1]) for k in range(8)]
+        factors = [[wide(p[:, k : k + 1]) for k in range(8)] for p in others]
         for k in range(8):
-            head = parts[0]
-            factors = [jnp.broadcast_to(p[:, k : k + 1], p.shape) for p in parts]
-            pivot = head[k : k + 1, :] / factors[0][k : k + 1, :]
-            parts = [p - f * pivot for p, f in zip(parts, factors)]
-            parts[0] = jnp.where(at == k, pivot, parts[0])
-        parts = [pltpu.roll(p, lanes - 8, 1) for p in parts]
-        return tuple(parts[1:] + parts[:1])
+            inverse = 1.0 / wide(columns[k][k : k + 1])
+            pivot = wide(head[k : k + 1]) * inverse
+            head = jnp.where(at == k, pivot, head - columns[k] * pivot)
+            for q in range(k + 1, 8):
+                entry = wide(columns[q][k : k + 1]) * inverse
+                columns[q] = jnp.where(at == k, entry, columns[q] - columns[k] * entry)
+        pivots = [wide(head[k : k + 1]) for k in range(8)]
+        parts = []
+        for p, f in zip(others, factors):
+            terms = [f[k] * pivots[k] for k in range(8)]
+            while len(terms) > 1:
+                terms = [x + y for x, y in zip(terms[::2], terms[1::2])]
+            parts.append(p - terms[0])
+        return tuple(pltpu.roll(p, lanes - 8, 1) for p in parts + [head])
 
     parts = tuple(system[8 * i : 8 * i + 8] for i in range(rows // 8))
     parts = lax.fori_loop(0, rows // 8, block, parts)
@@ -53,17 +67,26 @@
 
 def kernel(
     geometry,
+    prior_hbm,
+    kappa_hbm,
+    east_hbm,
+    north_hbm,
+    land_hbm,
+    owner_ref,
+    offset_hbm,
+    value_hbm,
+    var_hbm,
+    noise_hbm,
+    out_ref,
     prior_ref,
     kappa_ref,
     east_ref,
     north_ref,
     land_ref,
-    owner_ref,
     offset_ref,
     value_ref,
     var_ref,
     noise_ref,
-    out_ref,
     padded,
     middle,
     forecast,
@@ -89,6 +112,7 @@
     row_site,
     wet_cols,
     site_cols,
+    stage_sem,
     halo_send,
     halo_recv,
     reduce_send,
@@ -123,6 +147,25 @@
     def piece_of(d):
         return s - mine + lax.rem(mine + d, n_piece)
 
+    staged = [
+        pltpu.make_async_copy(source, target, stage_sem.at[i])
+        for i, (source, target) in enumerate(
+            (
+                (kappa_hbm, kappa_ref),
+                (east_hbm, east_ref),
+                (north_hbm, north_ref),
+                (land_hbm, land_ref),
+                (prior_hbm, prior_ref),
+                (offset_hbm, offset_ref),
+                (value_hbm, value_ref),
+                (var_hbm, var_ref),
+                (noise_hbm, noise_ref),
+            )
+        )
+    ]
+    for copy in staged:
+        copy.start()
+
     barrier = pltpu.get_barrier_semaphore()
     for d in range(1, n_slab):
         pl.semaphore_signal(barrier, inc=1, device_id=(slab_of(d), z), device_id_type=MESH)
@@ -133,6 +176,8 @@
         tile = prior_ref[:, pl.ds(r, 8), :]
         padded[pl.ds(r + 2, 8)] = jnp.swapaxes(tile, 0, 1)
 
+    for copy in staged[:5]:
+        copy.wait()
     wet = land_ref[...].astype(F32)
     ext[0, BASE : BASE + rows] = wet * kappa_ref[...]
     ext[1, BASE : BASE + rows] = wet
@@ -180,6 +225,8 @@
 
     lax.fori_loop(1, rows // 8 - 1, fill_rest, 0)
 
+    for copy in staged[5:]:
+        copy.wait()
     offsets = offset_ref[...]
     batch_at = lax.broadcasted_iota(jnp.int32, offsets.shape, 0)
     owner_rows = jnp.zeros(offsets.shape, jnp.int32)
@@ -189,25 +236,6 @@
     site_col = (offsets % width).astype(F32)
     sites[0:batches] = site_row
     sites[batches : 2 * batches] = site_col
-    flipped = sites[...].T
-    row0 = (s * rows).astype(F32)
-    col0 = (z * LANES).astype(F32)
-    columns = lax.broadcasted_iota(jnp.int32, (1, LANES), 1).astype(F32) + col0
-    for b in range(batches):
-        row_j = flipped[:, b : b + 1]
-        col_j = flipped[:, batches + b : batches + b + 1]
-        gap = col_j - columns
-        column_taper[b] = jnp.exp(-rate * (gap * gap))
-        row_site[b] = jnp.broadcast_to(row_j, (nobs, LANES)) - row0
-        for later in range(b + 1, batches):
-            g_row = row_j - sites[later : later + 1]
-            g_col = col_j - sites[batches + later : batches + later + 1]
-            tapers[b, :, nobs * later : nobs * (later + 1)] = jnp.exp(
-                -rate * (g_row * g_row + g_col * g_col)
-            )
-        base_misfit[b] = (
-            value_ref[b : b + 1] + jnp.sqrt(var_ref[b : b + 1]) * noise_ref[b].T
-        )
     line_of[...] = jnp.where(owner_rows == s * rows, offsets // width, -1)
     for b in range(batches):
         column = (offsets % width)[b : b + 1]
@@ -298,11 +326,11 @@
         parts[2, spot] = low
         return carry
 
-    lax.fori_loop(0, rows + 2, first_step, 0, unroll=2)
-    lax.fori_loop(0, rows // 2, second_step, 0)
-
     swaps = []
     for chunk in range(chunks):
+        done = chunk * rb + 2 if chunk else 0
+        lax.fori_loop(done, (chunk + 1) * rb + 2, first_step, 0, unroll=2)
+        lax.fori_loop(chunk * rb // 2, (chunk + 1) * rb // 2, second_step, 0)
         for d in range(1, n_mem):
             t = mem_of(d)
             swaps.append(
@@ -319,8 +347,9 @@
                     device_id_type=MESH,
                 )
             )
-    for copy in swaps:
-        copy.start()
+        if chunk < EARLY:
+            for copy in swaps[chunk * (n_mem - 1) :]:
+                copy.start()
     states[:, pl.ds(pl.multiple_of(z * OWN, OWN), OWN), :] = forecast[
         :, :, pl.ds(pl.multiple_of(z * LANES, LANES), LANES)
     ]
@@ -363,6 +392,17 @@
         )
     for copy in reduces:
         copy.start()
+    flipped = sites[...].T
+    for b in range(batches - 1):
+        row_j = flipped[:, b : b + 1]
+        col_j = flipped[:, batches + b : batches + b + 1]
+        for later in range(b + 1, batches):
+            g_row = row_j - sites[later : later + 1]
+            g_col = col_j - sites[batches + later : batches + later + 1]
+            tapers[b, :, nobs * later : nobs * (later + 1)] = jnp.exp(
+                -rate * (g_row * g_row + g_col * g_col)
+            )
+
     total = picked[mine]
     for d, copy in enumerate(reduces, 1):
         copy.wait_recv()
@@ -386,8 +426,19 @@
         copy.start()
     gathered[own_rows] = total[0:OWN]
     gathered[members : members + OWN] = total[OWN : 2 * OWN]
+    row0 = (s * rows).astype(F32)
+    col0 = (z * LANES).astype(F32)
+    columns = lax.broadcasted_iota(jnp.int32, (1, LANES), 1).astype(F32) + col0
+    for b in range(batches):
+        gap = flipped[:, batches + b : batches + b + 1] - columns
+        column_taper[b] = jnp.exp(-rate * (gap * gap))
+        row_site[b] = jnp.broadcast_to(flipped[:, b : b + 1], (nobs, LANES)) - row0
+        base_misfit[b] = value_ref[b : b + 1] + jnp.sqrt(var_ref[b : b + 1]) * noise_ref[b]
     for copy in rings:
         copy.wait_recv()
+
+    for copy in swaps[EARLY * (n_mem - 1) :]:
+        copy.start()
 
     own_lanes = pl.ds(pl.multiple_of(mine * LANES, LANES), LANES)
     shares = []
@@ -444,18 +495,23 @@
         for copy in swaps[chunk * (n_mem - 1) : (chunk + 1) * (n_mem - 1)]:
             copy.wait_recv()
         first = chunk * rb
-        wet_here = jnp.concatenate([wet_cols[first + q : first + q + 1] for q in range(rb)], 1)
+        wet_here = jnp.concatenate(
+            [wet_cols[first + q : first + q + 1] * math.exp(-rate * q * q) for q in range(rb)], 1
+        )
         here = jnp.concatenate([states[first + q] for q in range(rb)], 1)
 
         def assimilate(b, here):
             anomalies = here - jnp.mean(here, axis=0, keepdims=True)
             high, low = split(anomalies)
             covariance = quick(dcat[b], jnp.concatenate([high, low, high], 0))
-            taper = []
+            gap = row_site[b] - float(first)
+            step = jnp.exp((2.0 * rate) * gap)
+            taper = jnp.exp(-rate * (gap * gap)) * column_taper[b]
+            weighted = []
             for q in range(rb):
-                gap = row_site[b] - float(first + q)
-                taper.append(jnp.exp(-rate * (gap * gap)) * column_taper[b])
-            high, low = split(covariance * jnp.concatenate(taper, 1))
+                weighted.append(covariance[:, LANES * q : LANES * (q + 1)] * taper)
+                taper = taper * step
+            high, low = split(jnp.concatenate(weighted, 1))
             both = quick(wcat[b], high)
             change = both[:members] + both[members:] + quick(wcat[b, 0:members], low)
             return here + change * wet_here
@@ -496,13 +552,23 @@
     tall = rows + 2 * BASE
     vmem = pl.BlockSpec(memory_space=pltpu.VMEM)
     smem = pl.BlockSpec(memory_space=pltpu.SMEM)
+    hbm = pl.BlockSpec(memory_space=pltpu.HBM)
     dma = pltpu.SemaphoreType.DMA
     out = pl.pallas_call(
         functools.partial(kernel, geometry),
         out_shape=jax.ShapeDtypeStruct((members * rows, LANES), F32),
-        in_specs=[vmem] * 5 + [smem] + [vmem] * 4,
+        in_specs=[hbm] * 5 + [smem] + [hbm] * 4,
         out_specs=vmem,
         scratch_shapes=[
+            pltpu.VMEM((own, rows, width), F32),
+            pltpu.VMEM((rows, width), F32),
+            pltpu.VMEM((rows, width), F32),
+            pltpu.VMEM((rows, width), F32),
+            pltpu.VMEM((rows, width), jnp.int32),
+            pltpu.VMEM((batches, nobs), jnp.int32),
+            pltpu.VMEM((batches, nobs), F32),
+            pltpu.VMEM((batches, nobs), F32),
+            pltpu.VMEM((batches, members, nobs), F32),
             pltpu.VMEM((rows + 4, own, width), F32),
             pltpu.VMEM((rows + 2, own, width), F32),
             pltpu.VMEM((rows, own, width), F32),
@@ -528,6 +594,7 @@
             pltpu.VMEM((batches, nobs, LANES), F32),
             pltpu.VMEM((rows, LANES), F32),
             pltpu.VMEM((members + own, batches * nobs), F32),
+            dma((9,)),
             dma((4,)),
             dma((4,)),
             dma((n_slab,)),
@@ -540,7 +607,7 @@
             dma((chunks * n_mem,)),
         ],
         compiler_params=pltpu.CompilerParams(
-            collective_id=0, has_side_effects=True, vmem_limit_bytes=48 << 20
+            collective_id=0, has_side_effects=True, vmem_limit_bytes=60 << 20
         ),
     )(
         prior_concentrations,
@@ -552,7 +619,7 @@
         obs_offset,
         obs_value,
         obs_var,
-        obs_noise,
+        jnp.swapaxes(obs_noise, 1, 2),
     )
     return out.reshape(members, rows, LANES)
 

time: 141 us -> 83.3 us (0.59)
  the two profiles are of different devices: /device:TPU:1 before, /device:TPU:6 now
where the time goes in v2:
time: 83.3 us; the launch traced here: 82.2 us
  Pallas kernels  79.1 us (95%)
  local copies, waits for them, and re-layouts  3.16 us (4%)
    pallas_call x1, Pallas kernels, on_device(): pl.pallas_call(functools.partial(kernel, geometry), out_shape=jax.ShapeDt...  79.1 us
    unnamed x1, local copies, waits for them, and re-layouts  3.16 us

profile of v2, /device:TPU:6, one launch (start us, length us, event | category | flops | bytes accessed | tf_op | source)
XLA Modules:
  0.0 82.2 jit_solution(288178092616215053)
XLA Ops:
  0.0 79.1 %shard_map.100 = f32[4096,128]{1,0:T(8,128)} custom-call(f32[8,64,1024]{2,1,0:T(8,128)} %prior_hbm.1, f32[64,1024]{1,0:T(8,128)} %kappa_hbm.1, f32[64,1024]{1,0:T(8,128)} %east_hbm.1, f32[64,1024]{1,0:T(8,128)} %north_hbm.1, s32[64,1024]{1,0:T(8,128)} %land_hbm.1, s32[4]{0:T(128)} %owner_ref.1, s32[4,256]{1,0:T(4,128)} %offset_hbm.1, f32[4,256]{1,0:T(4,128)} %value_hbm.1, ...), custom_call_target="tpu_custom_call" | custom-call | tf_op jit(solution)/shard_map/pallas_call | solution.py:557
  79.1 3.2 %copy.12 = f32[64,64,128]{2,1,0:T(8,128)} copy(f32[64,64,128]{2,1,0:T(8,128)} %bitcast.2) | data formatting | bytes 4194304

commit v3 on v2

--- a/solution.py
+++ b/solution.py
@@ -14,7 +14,7 @@
 MESH = pl.DeviceIdType.MESH
 LANES = 128
 OWN = 8
-EARLY = 1
+EARLY = 4
 BASE = 8
 
 
@@ -44,13 +44,22 @@
         head, others = parts[0], parts[1:]
         columns = [wide(head[:, k : k + 1]) for k in range(8)]
         factors = [[wide(p[:, k : k + 1]) for k in range(8)] for p in others]
-        for k in range(8):
-            inverse = 1.0 / wide(columns[k][k : k + 1])
-            pivot = wide(head[k : k + 1]) * inverse
-            head = jnp.where(at == k, pivot, head - columns[k] * pivot)
-            for q in range(k + 1, 8):
-                entry = wide(columns[q][k : k + 1]) * inverse
-                columns[q] = jnp.where(at == k, entry, columns[q] - columns[k] * entry)
+        for k in range(0, 8, 2):
+            p, v = (wide(columns[k][r : r + 1]) for r in (k, k + 1))
+            u, w = (wide(columns[k + 1][r : r + 1]) for r in (k, k + 1))
+            inverse = 1.0 / (p * w - u * v)
+            p, u, v, w = p * inverse, u * inverse, v * inverse, w * inverse
+
+            def eliminate(x):
+                upper, lower = wide(x[k : k + 1]), wide(x[k + 1 : k + 2])
+                first = w * upper - u * lower
+                second = p * lower - v * upper
+                x = x - (columns[k] * first + columns[k + 1] * second)
+                return jnp.where(at == k, first, jnp.where(at == k + 1, second, x))
+
+            head = eliminate(head)
+            for q in range(k + 2, 8):
+                columns[q] = eliminate(columns[q])
         pivots = [wide(head[k : k + 1]) for k in range(8)]
         parts = []
         for p, f in zip(others, factors):
@@ -245,17 +254,6 @@
     sea[...] = wet.astype(BF16)
     wet_cols[...] = land_ref[:, pl.ds(pl.multiple_of(z * LANES, LANES), LANES)].astype(F32)
 
-    for copy in halo:
-        copy.wait()
-
-    low_ok = (s > 0).astype(F32)
-    high_ok = (s < n_slab - 1).astype(F32)
-    for field in range(4):
-        ext[field, BASE - 2 : BASE] = stat_recv[1, 2 * field : 2 * field + 2] * low_ok
-        ext[field, BASE + rows : BASE + rows + 2] = (
-            stat_recv[0, 2 * field : 2 * field + 2] * high_ok
-        )
-
     tall = ext.shape[1]
     lane = lax.broadcasted_iota(jnp.int32, (1, width), 1)
     not_last = (lane < width - 1).astype(F32)
@@ -289,10 +287,6 @@
         coef[3, where] = o * in_n[1:]
         coef[4, where] = o * out_n[:-1]
 
-    for first in range(0, rows, 8):
-        coefficients(BASE - 1 + first, 8)
-    coefficients(BASE - 2, 1)
-    coefficients(BASE + rows - 1, 1)
 
     def stencil(source, at, row):
         def c(i):
@@ -326,44 +320,87 @@
         parts[2, spot] = low
         return carry
 
-    swaps = []
-    for chunk in range(chunks):
-        done = chunk * rb + 2 if chunk else 0
-        lax.fori_loop(done, (chunk + 1) * rb + 2, first_step, 0, unroll=2)
+    swaps = {}
+
+    def advance(chunk):
+        start = 0 if chunk == 0 else chunk * rb + (0 if chunk == 1 else 2)
+        stop = rb if chunk == 0 else (chunk + 1) * rb + 2
+        lax.fori_loop(start, stop, first_step, 0, unroll=2)
         lax.fori_loop(chunk * rb // 2, (chunk + 1) * rb // 2, second_step, 0)
         for d in range(1, n_mem):
             t = mem_of(d)
-            swaps.append(
-                pltpu.make_async_remote_copy(
-                    src_ref=forecast.at[
-                        pl.ds(chunk * rb, rb), :, pl.ds(pl.multiple_of(t * LANES, LANES), LANES)
-                    ],
-                    dst_ref=states.at[
-                        pl.ds(chunk * rb, rb), pl.ds(pl.multiple_of(z * OWN, OWN), OWN), :
-                    ],
-                    send_sem=swap_send.at[chunk * n_mem + d],
-                    recv_sem=swap_recv.at[chunk * n_mem + d],
-                    device_id=(s, t),
-                    device_id_type=MESH,
+            swaps[chunk, d] = pltpu.make_async_remote_copy(
+                src_ref=forecast.at[
+                    pl.ds(chunk * rb, rb), :, pl.ds(pl.multiple_of(t * LANES, LANES), LANES)
+                ],
+                dst_ref=states.at[
+                    pl.ds(chunk * rb, rb), pl.ds(pl.multiple_of(z * OWN, OWN), OWN), :
+                ],
+                send_sem=swap_send.at[chunk * n_mem + d],
+                recv_sem=swap_recv.at[chunk * n_mem + d],
+                device_id=(s, t),
+                device_id_type=MESH,
+            )
+
+    order = [*range(1, chunks - 1), 0, chunks - 1]
+    steps = [(chunk, d) for chunk in order for d in range(1, n_mem)]
+    early = EARLY * (n_mem - 1) // 4
+    for first in range(8, rows - 8, 8):
+        coefficients(BASE - 1 + first, 8)
+    for chunk in order:
+        if chunk == 0:
+            for copy in halo:
+                copy.wait()
+
+            low_ok = (s > 0).astype(F32)
+            high_ok = (s < n_slab - 1).astype(F32)
+            for field in range(4):
+                ext[field, BASE - 2 : BASE] = stat_recv[1, 2 * field : 2 * field + 2] * low_ok
+                ext[field, BASE + rows : BASE + rows + 2] = (
+                    stat_recv[0, 2 * field : 2 * field + 2] * high_ok
                 )
-            )
-        if chunk < EARLY:
-            for copy in swaps[chunk * (n_mem - 1) :]:
-                copy.start()
+            for first in (0, rows - 8):
+                coefficients(BASE - 1 + first, 8)
+            coefficients(BASE - 2, 1)
+            coefficients(BASE + rows - 1, 1)
+        advance(chunk)
+        for step in steps[:early]:
+            if step[0] == chunk:
+                swaps[step].start()
     states[:, pl.ds(pl.multiple_of(z * OWN, OWN), OWN), :] = forecast[
         :, :, pl.ds(pl.multiple_of(z * LANES, LANES), LANES)
     ]
 
     per_batch = nobs // LANES
+
+    def reduce_to(t):
+        return pltpu.make_async_remote_copy(
+            src_ref=picked.at[lax.rem(t, n_piece)],
+            dst_ref=reduce_buf.at[s],
+            send_sem=reduce_send.at[t],
+            recv_sem=reduce_recv.at[s],
+            device_id=(t, z),
+            device_id_type=MESH,
+        )
+
+    def reduce_from(t):
+        return pltpu.make_async_remote_copy(
+            src_ref=picked.at[mine],
+            dst_ref=reduce_buf.at[t],
+            send_sem=reduce_send.at[t],
+            recv_sem=reduce_recv.at[t],
+            device_id=(t, z),
+            device_id_type=MESH,
+        )
 
     def pick_batch(b, carry):
         line = line_of[pl.ds(b, 1), :]
         chosen_column = column_of[b]
         tracer = jnp.zeros((OWN, nobs), F32)
+        at_line = lax.broadcasted_iota(jnp.int32, (rows, OWN, nobs), 0) == line[None]
         for part in range(3):
-            tracer_part = quick(parts[part], chosen_column).reshape(rows, OWN, nobs)
-            for r in range(rows):
-                tracer = tracer + jnp.where(line == r, tracer_part[r], 0.0)
+            part_here = quick(parts[part], chosen_column).reshape(rows, OWN, nobs)
+            tracer = tracer + jnp.sum(jnp.where(at_line, part_here, 0.0), axis=0)
         sea_part = quick(sea[...], chosen_column)
         at_row = lax.broadcasted_iota(jnp.int32, (rows, nobs), 0)
         found = jnp.sum(jnp.where(line == at_row, sea_part, 0.0), axis=0, keepdims=True)
@@ -373,25 +410,17 @@
             picked[b * per_batch + q, OWN : 2 * OWN] = jnp.broadcast_to(
                 found[:, lanes], (OWN, LANES)
             )
+            for group in range(0, n_slab, n_piece):
+                t = group + b * per_batch + q
+
+                @pl.when(t != s)
+                def _():
+                    reduce_to(t).start()
+
         return carry
 
     lax.fori_loop(0, batches, pick_batch, 0)
 
-    reduces = []
-    for d in range(1, n_slab):
-        t = slab_of(d)
-        reduces.append(
-            pltpu.make_async_remote_copy(
-                src_ref=picked.at[lax.rem(t, n_piece)],
-                dst_ref=reduce_buf.at[d],
-                send_sem=reduce_send.at[d],
-                recv_sem=reduce_recv.at[d],
-                device_id=(t, z),
-                device_id_type=MESH,
-            )
-        )
-    for copy in reduces:
-        copy.start()
     flipped = sites[...].T
     for b in range(batches - 1):
         row_j = flipped[:, b : b + 1]
@@ -404,9 +433,9 @@
             )
 
     total = picked[mine]
-    for d, copy in enumerate(reduces, 1):
-        copy.wait_recv()
-        total = total + reduce_buf[d]
+    for d in range(1, n_slab):
+        reduce_from(slab_of(d)).wait_recv()
+        total = total + reduce_buf[slab_of(d)]
     piece[...] = total
 
     own_rows = pl.ds(pl.multiple_of(z * OWN, OWN), OWN)
@@ -437,8 +466,8 @@
     for copy in rings:
         copy.wait_recv()
 
-    for copy in swaps[EARLY * (n_mem - 1) :]:
-        copy.start()
+    for step in steps[early:]:
+        swaps[step].start()
 
     own_lanes = pl.ds(pl.multiple_of(mine * LANES, LANES), LANES)
     shares = []
@@ -448,7 +477,7 @@
                 src_ref=gathered,
                 dst_ref=site_cols.at[:, own_lanes],
                 send_sem=share_send.at[d],
-                recv_sem=share_recv.at[d],
+                recv_sem=share_recv.at[mine],
                 device_id=(piece_of(d), z),
                 device_id_type=MESH,
             )
@@ -456,13 +485,27 @@
     for copy in shares:
         copy.start()
     site_cols[:, own_lanes] = gathered[...]
-    for copy in shares:
-        copy.wait_recv()
+
+    def wait_pieces(which):
+        for p in which:
+
+            @pl.when(p != mine)
+            def _():
+                pltpu.make_async_remote_copy(
+                    src_ref=gathered,
+                    dst_ref=site_cols.at[:, pl.ds(p * LANES, LANES)],
+                    send_sem=share_send.at[p],
+                    recv_sem=share_recv.at[p],
+                    device_id=(piece_of(1), z),
+                    device_id_type=MESH,
+                ).wait_recv()
+
 
     eye = (
         lax.broadcasted_iota(jnp.int32, (members, 2 * members), 0)
         == lax.broadcasted_iota(jnp.int32, (members, 2 * members), 1)
     ).astype(F32)
+    wait_pieces(range(per_batch))
     for b in range(batches):
         now = slice(nobs * b, nobs * (b + 1))
         priors = site_cols[0:members, now]
@@ -472,28 +515,32 @@
         system = contract(
             deviations * inverse_var, jnp.concatenate([deviations, misfit], 0), (1, 1)
         ) + eye * (members - 1.0)
+        high, low = split(deviations.T)
+        dcat[b] = jnp.concatenate([high, high, low], 1)
         solved = solve_spd(system)
+        if b == 0:
+            wait_pieces(range(per_batch, n_piece))
         weights = (misfit - contract(solved, deviations, (0, 0))) * (
             inverse_var * (1.0 / (members - 1))
         )
-        high, low = split(deviations.T)
-        dcat[b] = jnp.concatenate([high, high, low], 1)
         high, low = split(weights)
         wcat[b] = jnp.concatenate([high, low], 0)
         if b < batches - 1:
             rest = slice(nobs * (b + 1), total_obs)
             values = site_cols[0:members, rest]
             anomalies = values - jnp.mean(values, axis=0, keepdims=True)
-            covariance = contract(deviations, anomalies, (0, 0))
+            high, low = split(anomalies)
+            covariance = quick(dcat[b], jnp.concatenate([high, low, high], 0))
+            high, low = split(tapers[b, :, rest] * covariance)
+            both = quick(wcat[b], high)
+            change = both[:members] + both[members:] + quick(wcat[b, 0:members], low)
             site_cols[0:members, rest] = (
-                values
-                + contract(weights, tapers[b, :, rest] * covariance, (1, 0))
-                * site_cols[members : members + 1, rest]
-            )
-
-    for chunk in range(chunks):
-        for copy in swaps[chunk * (n_mem - 1) : (chunk + 1) * (n_mem - 1)]:
-            copy.wait_recv()
+                values + change * site_cols[members : members + 1, rest]
+            )
+
+    for chunk in order:
+        for d in range(1, n_mem):
+            swaps[chunk, d].wait_recv()
         first = chunk * rb
         wet_here = jnp.concatenate(
             [wet_cols[first + q : first + q + 1] * math.exp(-rate * q * q) for q in range(rb)], 1
@@ -522,13 +569,15 @@
                 :, LANES * q : LANES * (q + 1)
             ]
 
-    for copy in swaps + reduces + rings + shares:
+    for d in range(1, n_slab):
+        reduce_from(slab_of(d)).wait_send()
+    for copy in [*swaps.values(), *rings, *shares]:
         copy.wait_send()
 
 
 def geometry_of(mesh_shape, rows, batches, nobs):
     n_piece = batches * nobs // LANES
-    return mesh_shape["slab"], mesh_shape["mem"], n_piece, min(16, rows // 2)
+    return mesh_shape["slab"], mesh_shape["mem"], n_piece, rows // 4
 
 
 def on_device(

time: 83.3 us -> 79.2 us (0.951); the launches traced: 82.2 us -> 79.1 us
  Pallas kernels: 79.1 us -> 75.9 us
    pallas_call x1, Pallas kernels: 79.1 us -> 75.9 us  [on_device(): pl.pallas_call(functools.partial(kernel, geometry), out_shape=jax.ShapeDt...]
where the time goes in v3:
time: 79.2 us; the launch traced here: 79.1 us
  Pallas kernels  75.9 us (96%)
  local copies, waits for them, and re-layouts  3.16 us (4%)
    pallas_call x1, Pallas kernels, on_device(): pl.pallas_call(functools.partial(kernel, geometry), out_shape=jax.ShapeDt...  75.9 us
    unnamed x1, local copies, waits for them, and re-layouts  3.16 us

profile of v3, /device:TPU:6, one launch (start us, length us, event | category | flops | bytes accessed | tf_op | source)
XLA Modules:
  0.0 79.1 jit_solution(6132154776731028540)
XLA Ops:
  0.0 75.9 %shard_map.100 = f32[4096,128]{1,0:T(8,128)} custom-call(f32[8,64,1024]{2,1,0:T(8,128)} %prior_hbm.1, f32[64,1024]{1,0:T(8,128)} %kappa_hbm.1, f32[64,1024]{1,0:T(8,128)} %east_hbm.1, f32[64,1024]{1,0:T(8,128)} %north_hbm.1, s32[64,1024]{1,0:T(8,128)} %land_hbm.1, s32[4]{0:T(128)} %owner_ref.1, s32[4,256]{1,0:T(4,128)} %offset_hbm.1, f32[4,256]{1,0:T(4,128)} %value_hbm.1, ...), custom_call_target="tpu_custom_call" | custom-call | tf_op jit(solution)/shard_map/pallas_call | solution.py:606
  75.9 3.2 %copy.12 = f32[64,64,128]{2,1,0:T(8,128)} copy(f32[64,64,128]{2,1,0:T(8,128)} %bitcast.2) | data formatting | bytes 4194304

commit v4 on v3

--- a/solution.py
+++ b/solution.py
@@ -325,8 +325,8 @@
     def advance(chunk):
         start = 0 if chunk == 0 else chunk * rb + (0 if chunk == 1 else 2)
         stop = rb if chunk == 0 else (chunk + 1) * rb + 2
-        lax.fori_loop(start, stop, first_step, 0, unroll=2)
-        lax.fori_loop(chunk * rb // 2, (chunk + 1) * rb // 2, second_step, 0)
+        lax.fori_loop(start, stop, first_step, 0, unroll=8)
+        lax.fori_loop(chunk * rb // 2, (chunk + 1) * rb // 2, second_step, 0, unroll=4)
         for d in range(1, n_mem):
             t = mem_of(d)
             swaps[chunk, d] = pltpu.make_async_remote_copy(

time: 79.2 us -> 76.3 us (0.963)
  Pallas kernels: 75.9 us -> 73 us
    pallas_call x1, Pallas kernels: 75.9 us -> 73 us  [on_device(): pl.pallas_call(functools.partial(kernel, geometry), out_shape=jax.ShapeDt...]
where the time goes in v4:
time: 76.3 us; the launch traced here: 76.2 us
  Pallas kernels  73 us (96%)
  local copies, waits for them, and re-layouts  3.16 us (4%)
    pallas_call x1, Pallas kernels, on_device(): pl.pallas_call(functools.partial(kernel, geometry), out_shape=jax.ShapeDt...  73 us
    unnamed x1, local copies, waits for them, and re-layouts  3.16 us

profile of v4, /device:TPU:6, one launch (start us, length us, event | category | flops | bytes accessed | tf_op | source)
XLA Modules:
  0.0 76.2 jit_solution(3044875610835277441)
XLA Ops:
  0.0 73.0 %shard_map.100 = f32[4096,128]{1,0:T(8,128)} custom-call(f32[8,64,1024]{2,1,0:T(8,128)} %prior_hbm.1, f32[64,1024]{1,0:T(8,128)} %kappa_hbm.1, f32[64,1024]{1,0:T(8,128)} %east_hbm.1, f32[64,1024]{1,0:T(8,128)} %north_hbm.1, s32[64,1024]{1,0:T(8,128)} %land_hbm.1, s32[4]{0:T(128)} %owner_ref.1, s32[4,256]{1,0:T(4,128)} %offset_hbm.1, f32[4,256]{1,0:T(4,128)} %value_hbm.1, ...), custom_call_target="tpu_custom_call" | custom-call | tf_op jit(solution)/shard_map/pallas_call | solution.py:606
  73.0 3.2 %copy.12 = f32[64,64,128]{2,1,0:T(8,128)} copy(f32[64,64,128]{2,1,0:T(8,128)} %bitcast.2) | data formatting | bytes 4194304

commit v5 on v4

--- a/solution.py
+++ b/solution.py
@@ -14,7 +14,7 @@
 MESH = pl.DeviceIdType.MESH
 LANES = 128
 OWN = 8
-EARLY = 4
+EARLY = 5
 BASE = 8
 
 
@@ -466,8 +466,6 @@
     for copy in rings:
         copy.wait_recv()
 
-    for step in steps[early:]:
-        swaps[step].start()
 
     own_lanes = pl.ds(pl.multiple_of(mine * LANES, LANES), LANES)
     shares = []
@@ -484,6 +482,8 @@
         )
     for copy in shares:
         copy.start()
+    for step in steps[early:]:
+        swaps[step].start()
     site_cols[:, own_lanes] = gathered[...]
 
     def wait_pieces(which):

time: 76.3 us -> 75.8 us (level)
  no operation moved by 1% of the time
where the time goes in v5:
time: 75.8 us; the launch traced here: 75.7 us
  Pallas kernels  72.5 us (96%)
  local copies, waits for them, and re-layouts  3.16 us (4%)
    pallas_call x1, Pallas kernels, on_device(): pl.pallas_call(functools.partial(kernel, geometry), out_shape=jax.ShapeDt...  72.5 us
    unnamed x1, local copies, waits for them, and re-layouts  3.16 us

profile of v5, /device:TPU:6, one launch (start us, length us, event | category | flops | bytes accessed | tf_op | source)
XLA Modules:
  0.0 75.7 jit_solution(14480862396473181934)
XLA Ops:
  0.0 72.5 %shard_map.100 = f32[4096,128]{1,0:T(8,128)} custom-call(f32[8,64,1024]{2,1,0:T(8,128)} %prior_hbm.1, f32[64,1024]{1,0:T(8,128)} %kappa_hbm.1, f32[64,1024]{1,0:T(8,128)} %east_hbm.1, f32[64,1024]{1,0:T(8,128)} %north_hbm.1, s32[64,1024]{1,0:T(8,128)} %land_hbm.1, s32[4]{0:T(128)} %owner_ref.1, s32[4,256]{1,0:T(4,128)} %offset_hbm.1, f32[4,256]{1,0:T(4,128)} %value_hbm.1, ...), custom_call_target="tpu_custom_call" | custom-call | tf_op jit(solution)/shard_map/pallas_call | solution.py:606
  72.5 3.2 %copy.12 = f32[64,64,128]{2,1,0:T(8,128)} copy(f32[64,64,128]{2,1,0:T(8,128)} %bitcast.2) | data formatting | bytes 4194304

commit v6 on v5

--- a/solution.py
+++ b/solution.py
@@ -232,7 +232,7 @@
         fill(pl.multiple_of(8 * i, 8))
         return carry
 
-    lax.fori_loop(1, rows // 8 - 1, fill_rest, 0)
+    lax.fori_loop(1, rows // 8 - 1, fill_rest, 0, unroll=2)
 
     for copy in staged[5:]:
         copy.wait()
@@ -419,7 +419,7 @@
 
         return carry
 
-    lax.fori_loop(0, batches, pick_batch, 0)
+    lax.fori_loop(0, batches, pick_batch, 0, unroll=2)
 
     flipped = sites[...].T
     for b in range(batches - 1):

time: 75.8 us -> 76.3 us (level)
  no operation moved by 1% of the time
where the time goes in v6:
time: 76.3 us; the launch traced here: 76.2 us
  Pallas kernels  73 us (96%)
  local copies, waits for them, and re-layouts  3.16 us (4%)
    pallas_call x1, Pallas kernels, on_device(): pl.pallas_call(functools.partial(kernel, geometry), out_shape=jax.ShapeDt...  73 us
    unnamed x1, local copies, waits for them, and re-layouts  3.16 us

profile of v6, /device:TPU:6, one launch (start us, length us, event | category | flops | bytes accessed | tf_op | source)
XLA Modules:
  0.0 76.2 jit_solution(2986779758347567648)
XLA Ops:
  0.0 73.0 %shard_map.100 = f32[4096,128]{1,0:T(8,128)} custom-call(f32[8,64,1024]{2,1,0:T(8,128)} %prior_hbm.1, f32[64,1024]{1,0:T(8,128)} %kappa_hbm.1, f32[64,1024]{1,0:T(8,128)} %east_hbm.1, f32[64,1024]{1,0:T(8,128)} %north_hbm.1, s32[64,1024]{1,0:T(8,128)} %land_hbm.1, s32[4]{0:T(128)} %owner_ref.1, s32[4,256]{1,0:T(4,128)} %offset_hbm.1, f32[4,256]{1,0:T(4,128)} %value_hbm.1, ...), custom_call_target="tpu_custom_call" | custom-call | tf_op jit(solution)/shard_map/pallas_call | solution.py:606
  73.0 3.2 %copy.12 = f32[64,64,128]{2,1,0:T(8,128)} copy(f32[64,64,128]{2,1,0:T(8,128)} %bitcast.2) | data formatting | bytes 4194304
